TPU v7x, 256 devices: a whole 4x4x8 slice. The times are simulated.
256 devices in a mesh: dp: 16 (over x, y_hi, core), mp: 16 (over z, y_lo).
Axes of the slice: x: 4, y: 4 (y_hi: 2, y_lo: 2; y = y_hi * 2 + y_lo), z: 8, core: 2. Of those that a mesh axis runs over, the one named last changes fastest.
Arguments:
- tokens: bfloat16 [4096, 6144], P('dp', 'mp'), may hold values from -6 to 6
- ln_gain: bfloat16 [6144], replicated, may hold values from 0.25 to 1.75
- w_qkv: bfloat16 [6144, 32, 384], P(None, 'mp'), as said below
- q_gain: bfloat16 [128], replicated, may hold values from 0.25 to 1.75
- k_gain: bfloat16 [128], replicated, may hold values from 0.25 to 1.75
- d_out: bfloat16 [4096, 4096], P('dp', 'mp'), may hold values from -6 to 6
Outputs:
- attn_out: bfloat16 [4096, 4096], P('dp', 'mp')
- grad_tokens: bfloat16 [4096, 6144], P('dp', 'mp')
- grad_weight: float32 [6144, 32, 384], P('dp', 'mp')
Inputs may be any that keep to these rules, and one draw needn't show every extreme that they name: `w_qkv`: entries of order 6144 ** -0.5.
All inputs are finite; a program needn't handle non-finite values.
Results may differ from a plain program's by a relative error of at most 0.028.
Values may be sent and summed in bfloat16 or wider, within the bound.
No kernel may reach another device: no remote copies, remote signals or barrier semaphores. Data moves between devices by JAX's collectives and lax.ppermute only.
A program may use at most 128 MiB of HBM per device.

v0:
```python
import functools
import jax
import jax.numpy as jnp
from jax import lax
from jax.experimental import pallas as pl
from jax.experimental.pallas import tpu as pltpu
from jax.sharding import PartitionSpec as P

EPSILON = 1e-06
Z, YL, X, YH, CORES = 8, 2, 4, 2, 2
BF, F32 = jnp.bfloat16, jnp.float32
MIB = 1 << 20
GROUP = 16
EXTRA = 16
FAR = Z // 2
COST = pl.CostEstimate(flops=1024, bytes_accessed=1024, transcendentals=0)


def z_step(values, d):
    pairs = [(z * YL + y, ((z + d) % Z) * YL + y) for z in range(Z) for y in range(YL)]
    return lax.ppermute(values, "mp", pairs)


def yl_swap(values):
    return lax.ppermute(values, "mp", [(i, i ^ 1) for i in range(Z * YL)])


def x_step(values, d):
    n = YH * CORES
    pairs = [(x * n + r, ((x + d) % X) * n + r) for x in range(X) for r in range(n)]
    return lax.ppermute(values, "dp", pairs)


def yh_swap(values):
    return lax.ppermute(values, "dp", [(i, i ^ 2) for i in range(X * YH * CORES)])


def core_swap(values):
    return lax.ppermute(values, "dp", [(i, i ^ 1) for i in range(X * YH * CORES)])


def z_index():
    return lax.axis_index("mp") // YL


def yl_index():
    return lax.rem(lax.axis_index("mp"), YL)


def x_index():
    return lax.axis_index("dp") // (YH * CORES)


def yh_index():
    return lax.rem(lax.axis_index("dp") // CORES, YH)


def core_index():
    return lax.rem(lax.axis_index("dp"), CORES)


def held(shape, dtype):
    return pltpu.VMEM(shape, dtype)


def call(kernel, out_shape, *args, deps=(), hbm=(), limit=6, scratch=()):
    vmem, anywhere = pl.BlockSpec(memory_space=pltpu.VMEM), pl.BlockSpec(memory_space=pl.ANY)
    specs = [anywhere if i in hbm else vmem for i in range(len(args))]
    count = len(args)
    name = getattr(kernel, "func", kernel).__name__

    def body(*refs):
        kernel(*refs[:count], *refs[count + len(deps) :])

    return pl.pallas_call(
        body,
        in_specs=specs + [anywhere] * len(deps),
        out_specs=[vmem] * len(out_shape),
        out_shape=[(jax.ShapeDtypeStruct if o[2:] else held)(o[0], o[1]) for o in out_shape],
        scratch_shapes=list(scratch),
        compiler_params=pltpu.CompilerParams(vmem_limit_bytes=limit * MIB),
        cost_estimate=COST,
        name=name,
    )(*args, *deps)


def tie(values, dep, limit):
    anywhere = pl.BlockSpec(memory_space=pl.ANY)
    count = len(values)
    return pl.pallas_call(
        lambda *refs: None,
        in_specs=[anywhere] * (count + 1),
        out_specs=[anywhere] * count,
        out_shape=[jax.ShapeDtypeStruct(v.shape, v.dtype) for v in values],
        input_output_aliases={i: i for i in range(count)},
        compiler_params=pltpu.CompilerParams(vmem_limit_bytes=limit * MIB),
        cost_estimate=COST,
        name="tie",
    )(*values, dep)


def hold(ref, out_ref):
    out_ref[...] = ref[...]


def pair(*refs):
    count = len(refs) // 3
    for i, out_ref in enumerate(refs[2 * count :]):
        out_ref[0] = refs[2 * i][...]
        out_ref[1] = refs[2 * i + 1][...]


def load(source, out_ref, sems):
    groups = out_ref.shape[0] // Z
    copies = []
    for i in range(Z):
        part = pl.ds(i * groups, groups)
        copies.append(pltpu.make_async_copy(source.at[part], out_ref.at[part], sems.at[i]))
        copies[-1].start()
    for copy in copies:
        copy.wait()


def gather_tokens(tokens, w_qkv, *early):
    other = yl_swap(tokens)
    own_up, own_down = z_step(tokens, 1), z_step(tokens, -1)
    tokens = call(hold, [(tokens.shape, BF)], tokens, deps=[*early, other])[0]
    other_up, other_down = z_step(other, 1), z_step(other, -1)
    blocks, shape = {}, ((YL, *tokens.shape), BF)
    blocks[Z - 1], blocks[1] = call(pair, [shape] * 2, own_up, other_up, own_down, other_down)
    blocks[0] = call(pair, [shape], tokens, other, deps=[blocks[1]])[0]
    w = w_qkv.reshape(-1, GROUP, *w_qkv.shape[1:]).swapaxes(1, 2)
    for s in range(2, FAR):
        blocks[Z - s] = z_step(blocks[Z - s + 1], 1)
        blocks[s] = z_step(blocks[s - 1], -1)
        if s == 2:
            blocks[Z - s], blocks[s] = tie([blocks[Z - s], blocks[s]], w, 46)
        if s == 3:
            out, sems = [(w.shape, BF)], [pltpu.SemaphoreType.DMA((Z,))]
            deps = [blocks[2]]
            w = call(load, out, w, deps=deps, hbm=[0], limit=46, scratch=sems)[0]
            blocks[s] = tie([blocks[s]], w, 1)[0]
    blocks[FAR] = z_step(blocks[FAR + 1], 1)
    return [blocks[d] for d in range(Z)], w, tokens


def repeat(count, body):
    def step(i, carry):
        body(i)
        return carry

    lax.fori_loop(0, count, step, 0)


def entry(values, i):
    result = values[-1]
    for at, value in reversed(list(enumerate(values[:-1]))):
        result = jnp.where(i == at, value, result)
    return result


def joined(w_ref):
    heads, columns = w_ref.shape[1], w_ref.shape[3]
    return jnp.concatenate([w_ref[:, h].reshape(-1, columns) for h in range(heads)], 1)


def gains_at(gain_ref, d):
    z, yl = lax.rem(z_index() + d, Z), yl_index()
    return [gain_ref[z * YL + y] for y in (yl, 1 - yl)]


def w_at(w_ref, d):
    z, yl = lax.rem(z_index() + d, Z), yl_index()
    groups = w_ref.shape[0] // (Z * YL)
    firsts = [(z * YL + y) * groups for y in (yl, 1 - yl)]
    return jnp.concatenate([joined(w_ref.at[pl.ds(f, groups)]) for f in firsts], 0)


CHUNKS = 4


def row_sums(blocks, rows):
    size, width = blocks[0][0, rows].shape
    acc = jnp.zeros((size, width), F32)
    acc2 = jnp.zeros((size, width), F32)
    for block in blocks:
        for r in range(YL):
            v = block[r, rows].astype(F32)
            acc = acc + v
            acc2 = acc2 + v * v
    return jnp.sum(acc, 1, keepdims=True), jnp.sum(acc2, 1, keepdims=True)


def lanes(first, second, third):
    lane = lax.broadcasted_iota(jnp.int32, (first.shape[0], 128), 1)
    return jnp.where(lane == 0, first, jnp.where(lane == 1, second, third))


def centred(block, shift, gains):
    return jnp.concatenate(
        [((block[r].astype(F32) - shift) * g).astype(BF) for r, g in enumerate(gains)], 1
    )


def project_near(*refs):
    *blocks, gain_ref, w_ref, part_ref, wg_ref, sums_ref = refs
    rows, width = blocks[0].shape[1:]

    def chunk(i):
        at = pl.ds(pl.multiple_of(i * (rows // CHUNKS), rows // CHUNKS), rows // CHUNKS)
        total, square = row_sums(blocks, at)
        sums_ref[at] = lanes(total, square, total / (len(blocks) * YL * width))

    repeat(CHUNKS, chunk)
    shift = sums_ref[:, 2:3]
    part_ref[...] = jnp.zeros_like(part_ref)
    wg_ref[...] = jnp.zeros_like(wg_ref)
    for d in range(Z):
        gains = gains_at(gain_ref, d)
        left = jnp.broadcast_to(jnp.concatenate(gains, 1), (16, width * YL)).astype(BF)
        if d == FAR:
            wg_ref[...] += dot_nn(left, w_at(w_ref, d))
            continue
        block = blocks[d if d < FAR else d - 1]
        left = jnp.concatenate([centred(block, shift, gains), left], 0)
        product = dot_nn(left, w_at(w_ref, d))
        part_ref[...] += product[:rows]
        wg_ref[...] += product[rows:]


def project(*refs):
    blocks = refs[:Z]
    gain_ref, w_ref, part_ref, wg_ref, sums_ref, qkv_ref, own_ref, sib_ref, stats_ref = refs[Z:-1]
    both_ref = refs[-1]
    rows, width = blocks[0].shape[1:]
    cols = width * Z * YL
    total, square = row_sums([blocks[FAR]], slice(None))
    mean = (total + sums_ref[:, 0:1]) / cols
    inv = lax.rsqrt((square + sums_ref[:, 1:2]) / cols - mean * mean + EPSILON)
    shift = sums_ref[:, 2:3]
    both_ref[...] = lanes(mean, inv, 0.0)
    stats_ref[...] = both_ref[...].T[:8]
    gains = gains_at(gain_ref, FAR)
    product = dot_nn(centred(blocks[FAR], shift, gains), w_at(w_ref, FAR))
    qkv_ref[...] = inv * (part_ref[...] + product - (mean - shift) * wg_ref[0:1])
    first = core_index() == yl_index()

    def chunk(i):
        at = pl.ds(pl.multiple_of(i * (rows // CHUNKS), rows // CHUNKS), rows // CHUNKS)
        mean, inv = both_ref[at, 0:1], both_ref[at, 1:2]
        for d in range(Z):
            zd = lax.rem(z_index() + d, Z)
            parts = [
                ((blocks[d][r, at].astype(F32) - mean) * inv * g).astype(BF)
                for r, g in enumerate(gains_at(gain_ref, d))
            ]
            own_ref[zd, at] = jnp.where(first, parts[0], parts[1])
            sib_ref[zd, at] = jnp.where(first, parts[1], parts[0])

    repeat(CHUNKS, chunk)


def dot_nt(a, b):
    return lax.dot_general(a, b, (((1,), (1,)), ((), ())), preferred_element_type=F32)


def dot_tn(a, b):
    return lax.dot_general(a, b, (((0,), (0,)), ((), ())), preferred_element_type=F32)


def dot_nn(a, b):
    return jnp.dot(a, b, preferred_element_type=F32)


def head_norm(values):
    centred = values - jnp.mean(values, -1, keepdims=True)
    inv = lax.rsqrt(jnp.mean(centred * centred, -1, keepdims=True) + EPSILON)
    return centred * inv, inv


def norm_back(grad, gain, unit, inv):
    scaled = grad * gain
    return inv * (
        scaled
        - jnp.mean(scaled, -1, keepdims=True)
        - unit * jnp.mean(scaled * unit, -1, keepdims=True)
    )


def pack(sums):
    high = sums.astype(BF).astype(F32)
    return jnp.concatenate([high, sums - high], 0).astype(BF)


def unpack(extra):
    wide = extra.astype(F32)
    half = wide.shape[0] // 2
    return wide[:half] + wide[half:]


def attend(heads, hd, qkv_ref, wg_ref, gains_ref, do_ref, w_ref, *outs):
    out_ref, gt_ref, sums_ref, fwd_ref, bwd_ref = outs
    scale = hd ** (-0.5)
    q_gain, k_gain = gains_ref[0:1], gains_ref[1:2]
    rows = qkv_ref.shape[0]
    acc_sum = jnp.zeros((rows, hd), F32)
    acc_cross = jnp.zeros((rows, hd), F32)
    for h in range(heads):
        base = h * 3 * hd
        q, k, v = (qkv_ref[:, base + i * hd : base + (i + 1) * hd] for i in range(3))
        q_unit, q_inv = head_norm(q)
        k_unit, k_inv = head_norm(k)
        q_half = (q_unit * q_gain).astype(BF)
        k_half = (k_unit * k_gain).astype(BF)
        v_half = v.astype(BF)
        d_out = do_ref[:, h * hd : (h + 1) * hd]
        exps = jnp.exp(dot_nt(q_half, k_half) * scale)
        probs = exps / jnp.sum(exps, -1, keepdims=True)
        probs_half = probs.astype(BF)
        out_ref[:, h * hd : (h + 1) * hd] = dot_nn(probs_half, v_half).astype(BF)
        grad_probs = dot_nt(d_out, v_half)
        grad_value = dot_tn(probs_half, d_out)
        inner = jnp.sum(probs * grad_probs, -1, keepdims=True)
        grad_scores = (probs * (grad_probs - inner) * scale).astype(BF)
        grad_q = norm_back(dot_nn(grad_scores, k_half), q_gain, q_unit, q_inv)
        grad_k = norm_back(dot_tn(grad_scores, q_half), k_gain, k_unit, k_inv)
        for i, (part, source) in enumerate(((grad_q, q), (grad_k, k), (grad_value, v))):
            cols = slice(base + i * hd, base + (i + 1) * hd)
            half = part.astype(BF)
            gt_ref[cols, :] = half.T
            wide = half.astype(F32)
            acc_sum = acc_sum + wide * wg_ref[0:1, cols]
            acc_cross = acc_cross + wide * source
    sums = jnp.sum(acc_sum, -1, keepdims=True)
    cross = jnp.sum(acc_cross, -1, keepdims=True)
    lane = lax.broadcasted_iota(jnp.int32, (rows, hd), 1)
    both = jnp.where(lane == 0, sums, jnp.where(lane == 1, cross, 0.0))
    sums = both.T[:8]
    sums_ref[...] = sums
    extra = pack(sums)
    width = fwd_ref.shape[0] - extra.shape[0]
    term = term_at(w_ref, gt_ref, FAR)
    for ref, part in ((fwd_ref, term[:width]), (bwd_ref, term[width:])):
        ref[:width] = part
        ref[width:] = extra


def term_at(w_ref, gt_ref, d):
    groups = w_ref.shape[0] // Z
    start = lax.rem(z_index() + d, Z) * groups
    return dot_nn(joined(w_ref.at[pl.ds(start, groups)]), gt_ref[...]).astype(BF)


def relay_message(at, terms_ref, f_ref, b_ref, sums_ref, fwd_ref, bwd_ref):
    width = terms_ref.shape[1] // YL
    sums = sums_ref[...]
    whole = len(f_ref.shape) == 3
    for i, (got, ref) in enumerate(((f_ref, fwd_ref), (b_ref, bwd_ref))):
        for y in range(YL):
            term = terms_ref[at + i, y * width : (y + 1) * width]
            if whole or y == i:
                source = got.at[y] if whole else got
                ref[y, :width] = (term.astype(F32) + source[:width].astype(F32)).astype(BF)
                ref[y, width:] = pack(unpack(source[width:]) + sums)
            else:
                ref[y, :width] = term
                ref[y, width:] = pack(sums)


def swap_message(at, terms_ref, f_ref, b_ref, sums_ref, mine_ref, other_ref):
    width = terms_ref.shape[1] // YL
    yl = yl_index()
    for ref, y in ((mine_ref, yl), (other_ref, 1 - yl)):
        term = terms_ref[at, pl.ds(pl.multiple_of(y * width, width), width)]
        ref[:width] = wide_sum(term, f_ref[y, :width], b_ref[y, :width]).astype(BF)
        ref[width:] = pack(unpack(f_ref[y, width:]) + unpack(b_ref[y, width:]) + sums_ref[...])


def finish_tokens(mine_ref, other_ref, tok_ref, gain_ref, stats_ref, out_ref):
    rows, width = tok_ref.shape
    cols = width * Z * YL
    grad = wide_sum(mine_ref[:width], other_ref[:width]).T
    sums = (unpack(mine_ref[width:]) + unpack(other_ref[width:])).T / cols
    stats = stats_ref[...].T
    inv = stats[:, 1:2]
    scaled = grad * gain_ref[lax.axis_index("mp")]
    unit = (tok_ref[...].astype(F32) - stats[:, 0:1]) * inv
    out_ref[...] = (inv * (scaled - sums[:, 0:1] - unit * sums[:, 1:2])).astype(BF)


REST_DXS = (2, 1, 3, 0)


def weight_term(dx, h, left, own_ref, sib_ref):
    block = lax.rem(x_index() + dx, X) * YH + h
    right = jnp.concatenate([own_ref[block], sib_ref[block]], 0)
    return dot_nn(left, right).astype(BF)


def left_at(gt_ref, gs_ref, start, size):
    return jnp.concatenate([gt_ref[start : start + size], gs_ref[start : start + size]], 1)


def first_terms(own_ref, sib_ref, gt_ref, gs_ref, w_ref, fwd_ref, bwd_ref, other_ref, terms_ref):
    main, rest = fwd_ref.shape[0], other_ref.shape[1]
    left = left_at(gt_ref, gs_ref, 0, main)
    fwd_ref[...] = weight_term(2, 0, left, own_ref, sib_ref)
    bwd_ref[...] = weight_term(2, 1, left, own_ref, sib_ref)
    left = left_at(gt_ref, gs_ref, main, rest)
    for i, dx in enumerate(REST_DXS):
        other_ref[i] = weight_term(dx, 1 - yh_index(), left, own_ref, sib_ref)
    for i, d in enumerate((3, 5)):
        terms_ref[i] = term_at(w_ref, gt_ref, d)


def later_terms(own_ref, sib_ref, gt_ref, gs_ref, w_ref, near_ref, same_ref, terms_ref):
    main, rest = near_ref.shape[1], same_ref.shape[1]

    def near(i):
        left = left_at(gt_ref, gs_ref, 0, main)
        dx = entry((1, 3, 0), i // YH)
        near_ref[i] = weight_term(dx, lax.rem(i, YH), left, own_ref, sib_ref)

    def same(i):
        left = left_at(gt_ref, gs_ref, main, rest)
        same_ref[i] = weight_term(entry(REST_DXS, i), yh_index(), left, own_ref, sib_ref)

    def term(i):
        terms_ref[i] = term_at(w_ref, gt_ref, entry((2, 6, 1, 7, 0), i))

    repeat(near_ref.shape[0], near)
    repeat(same_ref.shape[0], same)
    repeat(terms_ref.shape[0], term)


def wide_sum(*parts):
    total = parts[0].astype(F32)
    for part in parts[1:]:
        total = total + part.astype(F32)
    return total


def main_message(near_ref, f_ref, b_ref, fwd_ref, bwd_ref):
    fwd_ref[0] = wide_sum(near_ref[0], f_ref[...]).astype(BF)
    fwd_ref[1] = near_ref[1]
    bwd_ref[0] = near_ref[2]
    bwd_ref[1] = wide_sum(near_ref[3], b_ref[...]).astype(BF)


def main_swap(near_ref, f_ref, b_ref, mine_ref, other_ref):
    yh = yh_index()
    other = 1 - yh
    mine_ref[...] = wide_sum(near_ref[4 + yh], f_ref[yh], b_ref[yh])
    other_ref[...] = wide_sum(near_ref[4 + other], f_ref[other], b_ref[other]).astype(BF)


def rest_first(own_ref, got_ref, fwd_ref, bwd_ref):
    half = fwd_ref.shape[0]
    fwd_ref[...] = wide_sum(own_ref[0, :half], got_ref[0, :half]).astype(BF)
    bwd_ref[...] = wide_sum(own_ref[0, half:], got_ref[0, half:]).astype(BF)


def rest_second(own_ref, got_ref, f_ref, b_ref, fwd_ref, bwd_ref):
    half = f_ref.shape[0]
    fwd_ref[:half] = wide_sum(own_ref[1, :half], got_ref[1, :half], f_ref[...]).astype(BF)
    fwd_ref[half:] = wide_sum(own_ref[1, half:], got_ref[1, half:]).astype(BF)
    bwd_ref[:half] = wide_sum(own_ref[2, :half], got_ref[2, :half]).astype(BF)
    bwd_ref[half:] = wide_sum(own_ref[2, half:], got_ref[2, half:], b_ref[...]).astype(BF)


def finish_weight(mine_ref, got_ref, own_ref, other_ref, f_ref, b_ref, out_ref, done_ref):
    done_ref[...] = jnp.zeros_like(done_ref)
    main, n3 = mine_ref.shape[0], out_ref.shape[2]
    parts = [
        wide_sum(mine_ref[...], got_ref[...]),
        wide_sum(own_ref[3], other_ref[3], f_ref[...], b_ref[...]),
    ]
    whole = jnp.concatenate(parts, 0)
    for h in range(out_ref.shape[1]):
        out_ref[:, h, :] = whole[h * n3 : (h + 1) * n3].T


def local(tokens, ln_gain, w_qkv, q_gain, k_gain, d_out):
    rows, width = tokens.shape
    heads, n3 = w_qkv.shape[1:]
    n = heads * n3
    hd = n3 // 3
    main = n // 2
    rest = n - main
    gains = ln_gain.astype(F32).reshape(Z * YL, 1, width)
    head_gains = jnp.stack([q_gain, k_gain]).astype(F32)

    with jax.named_scope("gather"):
        blocks, w, tokens = gather_tokens(tokens, w_qkv, gains, head_gains)
    blocks_shape = ((Z, rows, width), BF)
    eight = ((8, rows), F32)
    qkv_shape = ((rows, n), F32)
    near = blocks[:FAR] + blocks[FAR + 1 :]
    shape = [qkv_shape, ((16, n), F32), ((rows, 128), F32)]
    part, wg, row_part = call(project_near, shape, *near, gains, w, limit=12)
    shape = [qkv_shape, blocks_shape, blocks_shape, eight]
    operands = [*blocks, gains, w, part, wg, row_part]
    scratch = [pltpu.VMEM((rows, 128), F32)]
    qkv, own, for_sib, stats = call(project, shape, *operands, limit=12, scratch=scratch)
    with jax.named_scope("core_rows"):
        sib = core_swap(for_sib)
    half = ((width + EXTRA, rows), BF)
    full = ((YL, width + EXTRA, rows), BF)
    shape = [((rows, heads * hd), BF, None), ((n, rows), BF), eight, half, half]
    kernel = functools.partial(attend, heads, hd)
    attn_out, gt, sums, to_fwd, to_bwd = call(
        kernel, shape, qkv, wg, head_gains, d_out, w, limit=8
    )
    with jax.named_scope("core_grads"):
        gs = core_swap(gt)
    with jax.named_scope("z_relay1"):
        fwd, bwd = z_step(to_fwd, 1), z_step(to_bwd, -1)

    def relay(terms, at, fwd, bwd, *deps):
        kernel = functools.partial(relay_message, at)
        to_fwd, to_bwd = call(kernel, [full] * 2, terms, fwd, bwd, sums, deps=deps)
        return to_fwd, z_step(to_fwd, 1), z_step(to_bwd, -1)

    one, wide = ((main, width), BF), width * YL
    shape = [one, one, ((X, rest, width), BF), ((2, wide, rows), BF)]
    far_fwd, far_bwd, r_other, near_terms = call(first_terms, shape, own, sib, gt, gs, w)
    with jax.named_scope("x_main1"):
        w_fwd, w_bwd = x_step(far_fwd, 1), x_step(far_bwd, -1)
    with jax.named_scope("yh_rest"):
        r_got = yh_swap(r_other)
    with jax.named_scope("z_relay2"):
        sent, fwd, bwd = relay(near_terms, 0, fwd, bwd)
    shape = [((6, main, width), BF), ((X, rest, width), BF), ((5, wide, rows), BF)]
    w_near, r_own, terms = call(later_terms, shape, own, sib, gt, gs, w, deps=[sent])
    with jax.named_scope("x_main2"):
        message = ((YH, main, width), BF)
        to_fwd, to_bwd = call(main_message, [message] * 2, w_near, w_fwd, w_bwd)
        w_fwd, w_bwd = x_step(to_fwd, 1), x_step(to_bwd, -1)
    with jax.named_scope("z_relay3"):
        sent, fwd, bwd = relay(terms, 0, fwd, bwd, to_fwd)
    with jax.named_scope("z_relay4"):
        sent, fwd, bwd = relay(terms, 2, fwd, bwd)
    with jax.named_scope("x_rest1"):
        shape = [((rest // 2, width), BF)] * 2
        to_fwd, to_bwd = call(rest_first, shape, r_own, r_got, deps=[sent])
        r_fwd, r_bwd = x_step(to_fwd, 1), x_step(to_bwd, -1)
    with jax.named_scope("yh_main"):
        shape = [((main, width), F32), ((main, width), BF)]
        mine, other = call(main_swap, shape, w_near, w_fwd, w_bwd, deps=[to_fwd])
        got = yh_swap(other)
    with jax.named_scope("x_rest2"):
        shape = [((rest, width), BF)] * 2
        to_fwd, to_bwd = call(rest_second, shape, r_own, r_got, r_fwd, r_bwd, deps=[other])
        r_fwd, r_bwd = x_step(to_fwd, 1), x_step(to_bwd, -1)
    with jax.named_scope("y_tokens"):
        kernel = functools.partial(swap_message, 4)
        to_mine, to_other = call(kernel, [half] * 2, terms, fwd, bwd, sums, deps=[to_fwd])
        got_y = yl_swap(to_other)
    with jax.named_scope("weight_out"):
        shape = [((width, heads, n3), F32, None), ((8, 128), F32)]
        operands = [mine, got, r_own, r_got, r_fwd, r_bwd]
        grad_weight, done = call(finish_weight, shape, *operands, deps=[to_other])
    with jax.named_scope("tokens_out"):
        shape = [((rows, width), BF, None)]
        operands = [to_mine, got_y, tokens, gains, stats]
        grad_tokens = call(finish_tokens, shape, *operands, deps=[done])[0]
    return attn_out, grad_tokens, grad_weight


def solution(mesh):
    in_specs = (P("dp", "mp"), P(), P(None, "mp", None), P(), P(), P("dp", "mp"))
    out_specs = (P("dp", "mp"), P("dp", "mp"), P("dp", "mp", None))
    return jax.shard_map(local, mesh=mesh, in_specs=in_specs, out_specs=out_specs, check_vma=False)
```

profile of v0, /device:TPU:16, one launch (start us, length us, event | category | flops | bytes accessed | tf_op | source)
XLA Modules:
  0.0 113.1 jit_solution(16628649534971741673)
XLA Ops:
  2.0 5.9 %collective-permute-start.3 = (bf16[256,384]{1,0:T(8,128)(2,1)}, bf16[256,384]{1,0:T(8,128)(2,1)S(1)}, u32[]{:S(2)}, u32[]{:S(2)}) collective-permute-start(bf16[256,384]{1,0:T(8,128)(2,1)} %refs_0_.1), channel_id=1, source_target_pairs={{0,14},{1,15},{2,0},{3,1},{4,2},{5,3},{6,4},{7,5},{8,6},{9,7},{10,... | collective-permute-start | bytes 589832 | tf_op jit(solution)/shard_map/gather/ppermute | solution.py:21
  7.9 5.6 %collective-permute-start.4 = (bf16[256,384]{1,0:T(8,128)(2,1)S(1)}, bf16[256,384]{1,0:T(8,128)(2,1)S(1)}, u32[]{:S(2)}, u32[]{:S(2)}) collective-permute-start(bf16[256,384]{1,0:T(8,128)(2,1)S(1)} %collective-permute-done.refs_3_.refs_1_), channel_id=1, source_target_pairs={{0,14},{1,15},{2,0},{3,1},{4,2},{5,3},{6,4},{7,5},{8,6},{9,7},{10,... | collective-permute-start | bytes 589832 | tf_op jit(solution)/shard_map/gather/ppermute | solution.py:21
  16.7 3.6 %collective-permute-done.2.refs_1_ = bf16[256,384]{1,0:T(8,128)(2,1)S(1)} collective-permute-done((bf16[256,384]{1,0:T(8,128)(2,1)S(1)}, bf16[256,384]{1,0:T(8,128)(2,1)S(1)}, u32[]{:S(2)}, u32[]{:S(2)}) %collective-permute-start.2) | collective-permute-done | bytes 196640 | tf_op jit(solution)/shard_map/gather/ppermute | solution.py:21
  20.5 3.2 %collective-permute-start.6 = (bf16[2,256,384]{2,1,0:T(8,128)(2,1)S(1)}, bf16[2,256,384]{2,1,0:T(8,128)(2,1)S(1)}, u32[]{:S(2)}, u32[]{:S(2)}) collective-permute-start(bf16[2,256,384]{2,1,0:T(8,128)(2,1)S(1)} %get-tuple-element.44.refs_2_.refs_1_), channel_id=1, source_target_pairs={{0,14},{1,15},{2,0},{3,1},{4,2},{5,3},{6,4},{7,5},{8,6},{9,7},{10,... | collective-permute-start | bytes 1179656 | tf_op jit(solution)/shard_map/gather/ppermute | solution.py:21
  23.7 9.0 %copy.17 = bf16[384,16,2,384]{3,1,2,0:T(8,128)(2,1)} copy(bf16[384,16,2,384]{3,2,1,0:T(2,128)(2,1)} %bitcast.13) | data formatting | bytes 18874368 | tf_op jit(solution)/shard_map/gather/reshape | solution.py:132
  32.8 3.2 %collective-permute-start.7 = (bf16[2,256,384]{2,1,0:T(8,128)(2,1)S(1)}, bf16[2,256,384]{2,1,0:T(8,128)(2,1)S(1)}, u32[]{:S(2)}, u32[]{:S(2)}) collective-permute-start(bf16[2,256,384]{2,1,0:T(8,128)(2,1)S(1)} %get-tuple-element.46.refs_1_.refs_2_), channel_id=1, source_target_pairs={{0,14},{1,15},{2,0},{3,1},{4,2},{5,3},{6,4},{7,5},{8,6},{9,7},{10,... | collective-permute-start | bytes 1179656 | tf_op jit(solution)/shard_map/gather/ppermute | solution.py:21
  36.1 6.0 %collective-permute-done.8.refs_4_.refs_5_ = bf16[2,256,384]{2,1,0:T(8,128)(2,1)S(1)} collective-permute-done((bf16[2,256,384]{2,1,0:T(8,128)(2,1)S(1)}, bf16[2,256,384]{2,1,0:T(8,128)(2,1)S(1)}, u32[]{:S(2)}, u32[]{:S(2)}) %collective-permute-start.8) | collective-permute-done | bytes 393248 | tf_op jit(solution)/shard_map/gather/ppermute | solution.py:21
  42.2 3.8 %load.1.refs_1_.refs_8_.refs_9_.refs_4_ = bf16[384,2,16,384]{3,2,1,0:T(8,128)(2,1)S(1)} custom-call(bf16[384,2,16,384]{3,2,1,0:T(8,128)(2,1)} %bitcast.12, bf16[2,256,384]{2,1,0:T(8,128)(2,1)} %copy-done), custom_call_target="tpu_custom_call" | custom-call | flops 1024 | bytes 1024 | tf_op jit(solution)/shard_map/gather/load/pallas_call | solution.py:75
  47.0 3.8 %project_near.1 = (f32[256,768]{1,0:T(8,128)S(1)}, f32[16,768]{1,0:T(8,128)S(1)}, f32[256,128]{1,0:T(8,128)S(1)}) custom-call(bf16[2,256,384]{2,1,0:T(8,128)(2,1)S(1)} %pair.3.refs_0_, bf16[2,256,384]{2,1,0:T(8,128)(2,1)S(1)} %get-tuple-element.44.refs_2_.refs_1_, bf16[2,256,384]{2,1,0:T(8,128)(2,1)S(1)} %copy-done.1, bf16[2,256,384]{2,1,0:T(8,128)(2,1)S(1)} %tie.3.refs_3_, ...), custom_call_target="tpu_custom_call" | custom-call | flops 1024 | bytes 1024 | tf_op jit(solution)/shard_map/project_near/pallas_call | solution.py:75
  51.1 2.3 %project.1 = (f32[256,768]{1,0:T(8,128)S(1)}, bf16[8,256,384]{2,1,0:T(8,128)(2,1)S(1)}, bf16[8,256,384]{2,1,0:T(8,128)(2,1)S(1)}, f32[8,256]{1,0:T(8,128)S(1)}) custom-call(bf16[2,256,384]{2,1,0:T(8,128)(2,1)S(1)} %pair.3.refs_0_, bf16[2,256,384]{2,1,0:T(8,128)(2,1)S(1)} %get-tuple-element.44.refs_2_.refs_1_, bf16[2,256,384]{2,1,0:T(8,128)(2,1)S(1)} %copy-done.1, ...), custom_call_target="tpu_custom_call" | custom-call | flops 1024 | bytes 1024 | tf_op jit(solution)/shard_map/project/pallas_call | solution.py:75
  53.5 2.5 %attend.1 = (bf16[256,256]{1,0:T(8,128)(2,1)}, bf16[768,256]{1,0:T(8,128)(2,1)S(1)}, f32[8,256]{1,0:T(8,128)S(1)}, bf16[400,256]{1,0:T(8,128)(2,1)S(1)}, bf16[400,256]{1,0:T(8,128)(2,1)S(1)}) custom-call(f32[256,768]{1,0:T(8,128)S(1)} %get-tuple-element.51.refs_0_, f32[16,768]{1,0:T(8,128)S(1)} %get-tuple-element.49.refs_11_.refs_1_, ...), custom_call_target="tpu_custom_call" | custom-call | flops 1024 | bytes 1024 | tf_op jit(solution)/shard_map/attend/pallas_call | solution.py:75
  56.5 3.2 %collective-permute-start.13 = (bf16[400,256]{1,0:T(8,128)(2,1)S(1)}, bf16[400,256]{1,0:T(8,128)(2,1)S(1)}, u32[]{:S(2)}, u32[]{:S(2)}) collective-permute-start(bf16[400,256]{1,0:T(8,128)(2,1)S(1)} %get-tuple-element.58), channel_id=1, source_target_pairs={{0,14},{1,15},{2,0},{3,1},{4,2},{5,3},{6,4},{7,5},{8,6},{9,7},{10,... | collective-permute-start | bytes 614408 | tf_op jit(solution)/shard_map/z_relay1/ppermute | solution.py:21
  59.7 2.0 %first_terms.1 = (bf16[384,384]{1,0:T(8,128)(2,1)S(1)}, bf16[384,384]{1,0:T(8,128)(2,1)S(1)}, bf16[4,384,384]{2,1,0:T(8,128)(2,1)S(1)}, bf16[2,768,256]{2,1,0:T(8,128)(2,1)S(1)}) custom-call(bf16[8,256,384]{2,1,0:T(8,128)(2,1)S(1)} %get-tuple-element.53.refs_0_, bf16[8,256,384]{2,1,0:T(8,128)(2,1)S(1)} %collective-permute-done.10.refs_1_, ...), custom_call_target="tpu_custom_call" | custom-call | flops 1024 | bytes 1024 | tf_op jit(solution)/shard_map/first_terms/pallas_call | solution.py:75
  62.1 2.6 %collective-permute-done.12.refs_1_ = bf16[400,256]{1,0:T(8,128)(2,1)S(1)} collective-permute-done((bf16[400,256]{1,0:T(8,128)(2,1)S(1)}, bf16[400,256]{1,0:T(8,128)(2,1)S(1)}, u32[]{:S(2)}, u32[]{:S(2)}) %collective-permute-start.12) | collective-permute-done | bytes 204832 | tf_op jit(solution)/shard_map/z_relay1/ppermute | solution.py:21
  64.8 3.0 %collective-permute-start.15 = (bf16[2,400,256]{2,1,0:T(8,128)(2,1)S(1)}, bf16[2,400,256]{2,1,0:T(8,128)(2,1)S(1)}, u32[]{:S(2)}, u32[]{:S(2)}) collective-permute-start(bf16[2,400,256]{2,1,0:T(8,128)(2,1)S(1)} %get-tuple-element.62), channel_id=1, source_target_pairs={{0,14},{1,15},{2,0},{3,1},{4,2},{5,3},{6,4},{7,5},{8,6},{9,7},{10,... | collective-permute-start | bytes 1228808 | tf_op jit(solution)/shard_map/z_relay2/ppermute | solution.py:21
  71.1 6.3 %later_terms.1 = (bf16[6,384,384]{2,1,0:T(8,128)(2,1)S(1)}, bf16[4,384,384]{2,1,0:T(8,128)(2,1)S(1)}, bf16[5,768,256]{2,1,0:T(8,128)(2,1)S(1)}) custom-call(bf16[8,256,384]{2,1,0:T(8,128)(2,1)S(1)} %get-tuple-element.53.refs_0_, bf16[8,256,384]{2,1,0:T(8,128)(2,1)S(1)} %collective-permute-done.10.refs_1_, bf16[768,256]{1,0:T(8,128)(2,1)S(1)} %get-tuple-element.55.refs_2_, ...), custom_call_target="tpu_custom_call" | custom-call | flops 1024 | bytes 1024 | tf_op jit(solution)/shard_map/later_terms/pallas_call | solution.py:75
  77.6 2.2 %collective-permute-start.26 = (bf16[2,384,384]{2,1,0:T(8,128)(2,1)S(1)}, bf16[2,384,384]{2,1,0:T(8,128)(2,1)S(1)}, u32[]{:S(2)}, u32[]{:S(2)}) collective-permute-start(bf16[2,384,384]{2,1,0:T(8,128)(2,1)S(1)} %get-tuple-element.75), channel_id=1, source_target_pairs={{0,192},{16,208},{32,224},{48,240},{64,0},{80,16},{96,32},{112,48}... | collective-permute-start | bytes 1769480 | tf_op jit(solution)/shard_map/x_main2/ppermute | solution.py:31
  80.1 3.2 %collective-permute-start.19 = (bf16[2,400,256]{2,1,0:T(8,128)(2,1)S(1)}, bf16[2,400,256]{2,1,0:T(8,128)(2,1)S(1)}, u32[]{:S(2)}, u32[]{:S(2)}) collective-permute-start(bf16[2,400,256]{2,1,0:T(8,128)(2,1)S(1)} %get-tuple-element.68), channel_id=1, source_target_pairs={{0,14},{1,15},{2,0},{3,1},{4,2},{5,3},{6,4},{7,5},{8,6},{9,7},{10,... | collective-permute-start | bytes 1228808 | tf_op jit(solution)/shard_map/z_relay3/ppermute | solution.py:21
  84.0 5.8 %collective-permute-done.18.refs_1_ = bf16[2,400,256]{2,1,0:T(8,128)(2,1)S(1)} collective-permute-done((bf16[2,400,256]{2,1,0:T(8,128)(2,1)S(1)}, bf16[2,400,256]{2,1,0:T(8,128)(2,1)S(1)}, u32[]{:S(2)}, u32[]{:S(2)}) %collective-permute-start.18) | collective-permute-done | bytes 409632 | tf_op jit(solution)/shard_map/z_relay3/ppermute | solution.py:21
  90.0 3.1 %collective-permute-start.21 = (bf16[2,400,256]{2,1,0:T(8,128)(2,1)S(1)}, bf16[2,400,256]{2,1,0:T(8,128)(2,1)S(1)}, u32[]{:S(2)}, u32[]{:S(2)}) collective-permute-start(bf16[2,400,256]{2,1,0:T(8,128)(2,1)S(1)} %get-tuple-element.70), channel_id=1, source_target_pairs={{0,14},{1,15},{2,0},{3,1},{4,2},{5,3},{6,4},{7,5},{8,6},{9,7},{10,... | collective-permute-start | bytes 1228808 | tf_op jit(solution)/shard_map/z_relay4/ppermute | solution.py:21
  93.2 2.5 %collective-permute-start.24 = (bf16[192,384]{1,0:T(8,128)(2,1)S(1)}, bf16[192,384]{1,0:T(8,128)(2,1)S(1)}, u32[]{:S(2)}, u32[]{:S(2)}) collective-permute-start(bf16[192,384]{1,0:T(8,128)(2,1)S(1)} %get-tuple-element.74), channel_id=1, source_target_pairs={{0,192},{16,208},{32,224},{48,240},{64,0},{80,16},{96,32},{112,48}... | collective-permute-start | bytes 442376 | tf_op jit(solution)/shard_map/x_rest1/ppermute | solution.py:31
  98.4 3.7 %collective-permute-done.23.refs_2_ = bf16[192,384]{1,0:T(8,128)(2,1)S(1)} collective-permute-done((bf16[192,384]{1,0:T(8,128)(2,1)S(1)}, bf16[192,384]{1,0:T(8,128)(2,1)S(1)}, u32[]{:S(2)}, u32[]{:S(2)}) %collective-permute-start.23) | collective-permute-done | bytes 147488 | tf_op jit(solution)/shard_map/x_rest1/ppermute | solution.py:31
  102.4 2.0 %collective-permute-start.29 = (bf16[384,384]{1,0:T(8,128)(2,1)S(1)}, bf16[384,384]{1,0:T(8,128)(2,1)S(1)}, u32[]{:S(2)}, u32[]{:S(2)}) collective-permute-start(bf16[384,384]{1,0:T(8,128)(2,1)S(1)} %get-tuple-element.77.refs_4_), channel_id=1, source_target_pairs={{0,64},{16,80},{32,96},{48,112},{64,128},{80,144},{96,160},{112,17... | collective-permute-start | bytes 884744 | tf_op jit(solution)/shard_map/x_rest2/ppermute | solution.py:31
  105.9 1.9 %collective-permute-done.28.refs_1_ = bf16[384,384]{1,0:T(8,128)(2,1)S(1)} collective-permute-done((bf16[384,384]{1,0:T(8,128)(2,1)S(1)}, bf16[384,384]{1,0:T(8,128)(2,1)S(1)}, u32[]{:S(2)}, u32[]{:S(2)}) %collective-permute-start.28) | collective-permute-done | bytes 294944 | tf_op jit(solution)/shard_map/yh_main/ppermute | solution.py:35
  (76 shorter events, 21.8 us)
Async XLA Ops:
  2.0 11.4 %collective-permute-start.3 = (bf16[256,384]{1,0:T(8,128)(2,1)}, bf16[256,384]{1,0:T(8,128)(2,1)S(1)}, u32[]{:S(2)}, u32[]{:S(2)}) collective-permute-start(bf16[256,384]{1,0:T(8,128)(2,1)} %refs_0_.1), channel_id=1, source_target_pairs={{0,14},{1,15},{2,0},{3,1},{4,2},{5,3},{6,4},{7,5},{8,6},{9,7},{10,... | collective-permute-start | bytes 589832 | tf_op jit(solution)/shard_map/gather/ppermute | solution.py:21
  7.9 7.5 %collective-permute-start.1 = (bf16[256,384]{1,0:T(8,128)(2,1)}, bf16[256,384]{1,0:T(8,128)(2,1)S(1)}, u32[]{:S(2)}, u32[]{:S(2)}) collective-permute-start(bf16[256,384]{1,0:T(8,128)(2,1)} %refs_0_.1), channel_id=1, source_target_pairs={{0,2},{1,3},{2,4},{3,5},{4,6},{5,7},{6,8},{7,9},{8,10},{9,11},{10,... | collective-permute-start | bytes 589832 | tf_op jit(solution)/shard_map/gather/ppermute | solution.py:21
  7.9 8.9 %collective-permute-start.4 = (bf16[256,384]{1,0:T(8,128)(2,1)S(1)}, bf16[256,384]{1,0:T(8,128)(2,1)S(1)}, u32[]{:S(2)}, u32[]{:S(2)}) collective-permute-start(bf16[256,384]{1,0:T(8,128)(2,1)S(1)} %collective-permute-done.refs_3_.refs_1_), channel_id=1, source_target_pairs={{0,14},{1,15},{2,0},{3,1},{4,2},{5,3},{6,4},{7,5},{8,6},{9,7},{10,... | collective-permute-start | bytes 589832 | tf_op jit(solution)/shard_map/gather/ppermute | solution.py:21
  20.4 12.3 %collective-permute-start.5 = (bf16[2,256,384]{2,1,0:T(8,128)(2,1)S(1)}, bf16[2,256,384]{2,1,0:T(8,128)(2,1)S(1)}, u32[]{:S(2)}, u32[]{:S(2)}) collective-permute-start(bf16[2,256,384]{2,1,0:T(8,128)(2,1)S(1)} %get-tuple-element.45.refs_6_.refs_7_), channel_id=1, source_target_pairs={{0,2},{1,3},{2,4},{3,5},{4,6},{5,7},{6,8},{7,9},{8,10},{9,11},{10,... | collective-permute-start | bytes 1179656 | tf_op jit(solution)/shard_map/gather/ppermute | solution.py:21
  20.5 12.2 %collective-permute-start.6 = (bf16[2,256,384]{2,1,0:T(8,128)(2,1)S(1)}, bf16[2,256,384]{2,1,0:T(8,128)(2,1)S(1)}, u32[]{:S(2)}, u32[]{:S(2)}) collective-permute-start(bf16[2,256,384]{2,1,0:T(8,128)(2,1)S(1)} %get-tuple-element.44.refs_2_.refs_1_), channel_id=1, source_target_pairs={{0,14},{1,15},{2,0},{3,1},{4,2},{5,3},{6,4},{7,5},{8,6},{9,7},{10,... | collective-permute-start | bytes 1179656 | tf_op jit(solution)/shard_map/gather/ppermute | solution.py:21
  32.7 9.4 %collective-permute-start.8 = (bf16[2,256,384]{2,1,0:T(8,128)(2,1)S(1)}, bf16[2,256,384]{2,1,0:T(8,128)(2,1)S(1)}, u32[]{:S(2)}, u32[]{:S(2)}) collective-permute-start(bf16[2,256,384]{2,1,0:T(8,128)(2,1)S(1)} %get-tuple-element.47.refs_5_.refs_6_), channel_id=1, source_target_pairs={{0,2},{1,3},{2,4},{3,5},{4,6},{5,7},{6,8},{7,9},{8,10},{9,11},{10,... | collective-permute-start | bytes 1179656 | tf_op jit(solution)/shard_map/gather/ppermute | solution.py:21
  32.8 13.2 %collective-permute-start.7 = (bf16[2,256,384]{2,1,0:T(8,128)(2,1)S(1)}, bf16[2,256,384]{2,1,0:T(8,128)(2,1)S(1)}, u32[]{:S(2)}, u32[]{:S(2)}) collective-permute-start(bf16[2,256,384]{2,1,0:T(8,128)(2,1)S(1)} %get-tuple-element.46.refs_1_.refs_2_), channel_id=1, source_target_pairs={{0,14},{1,15},{2,0},{3,1},{4,2},{5,3},{6,4},{7,5},{8,6},{9,7},{10,... | collective-permute-start | bytes 1179656 | tf_op jit(solution)/shard_map/gather/ppermute | solution.py:21
  42.1 9.0 %collective-permute-start.9 = (bf16[2,256,384]{2,1,0:T(8,128)(2,1)S(1)}, bf16[2,256,384]{2,1,0:T(8,128)(2,1)S(1)}, u32[]{:S(2)}, u32[]{:S(2)}) collective-permute-start(bf16[2,256,384]{2,1,0:T(8,128)(2,1)S(1)} %collective-permute-done.8.refs_4_.refs_5_), channel_id=1, source_target_pairs={{0,2},{1,3},{2,4},{3,5},{4,6},{5,7},{6,8},{7,9},{8,10},{9,11},{10,... | collective-permute-start | bytes 1179656 | tf_op jit(solution)/shard_map/gather/ppermute | solution.py:21
  56.5 8.2 %collective-permute-start.12 = (bf16[400,256]{1,0:T(8,128)(2,1)S(1)}, bf16[400,256]{1,0:T(8,128)(2,1)S(1)}, u32[]{:S(2)}, u32[]{:S(2)}) collective-permute-start(bf16[400,256]{1,0:T(8,128)(2,1)S(1)} %get-tuple-element.57), channel_id=1, source_target_pairs={{0,2},{1,3},{2,4},{3,5},{4,6},{5,7},{6,8},{7,9},{8,10},{9,11},{10,... | collective-permute-start | bytes 614408 | tf_op jit(solution)/shard_map/z_relay1/ppermute | solution.py:21
  56.5 8.2 %collective-permute-start.13 = (bf16[400,256]{1,0:T(8,128)(2,1)S(1)}, bf16[400,256]{1,0:T(8,128)(2,1)S(1)}, u32[]{:S(2)}, u32[]{:S(2)}) collective-permute-start(bf16[400,256]{1,0:T(8,128)(2,1)S(1)} %get-tuple-element.58), channel_id=1, source_target_pairs={{0,14},{1,15},{2,0},{3,1},{4,2},{5,3},{6,4},{7,5},{8,6},{9,7},{10,... | collective-permute-start | bytes 614408 | tf_op jit(solution)/shard_map/z_relay1/ppermute | solution.py:21
  61.7 31.4 %collective-permute-start.22 = (bf16[4,384,384]{2,1,0:T(8,128)(2,1)S(1)}, bf16[4,384,384]{2,1,0:T(8,128)(2,1)S(1)}, u32[]{:S(2)}, u32[]{:S(2)}) collective-permute-start(bf16[4,384,384]{2,1,0:T(8,128)(2,1)S(1)} %get-tuple-element.72), channel_id=1, source_target_pairs={{0,32},{16,48},{32,0},{48,16},{64,96},{80,112},{96,64},{112,80},{1... | collective-permute-start | bytes 3538952 | tf_op jit(solution)/shard_map/yh_rest/ppermute | solution.py:35
  64.8 15.0 %collective-permute-start.15 = (bf16[2,400,256]{2,1,0:T(8,128)(2,1)S(1)}, bf16[2,400,256]{2,1,0:T(8,128)(2,1)S(1)}, u32[]{:S(2)}, u32[]{:S(2)}) collective-permute-start(bf16[2,400,256]{2,1,0:T(8,128)(2,1)S(1)} %get-tuple-element.62), channel_id=1, source_target_pairs={{0,14},{1,15},{2,0},{3,1},{4,2},{5,3},{6,4},{7,5},{8,6},{9,7},{10,... | collective-permute-start | bytes 1228808 | tf_op jit(solution)/shard_map/z_relay2/ppermute | solution.py:21
  67.8 11.9 %collective-permute-start.14 = (bf16[2,400,256]{2,1,0:T(8,128)(2,1)S(1)}, bf16[2,400,256]{2,1,0:T(8,128)(2,1)S(1)}, u32[]{:S(2)}, u32[]{:S(2)}) collective-permute-start(bf16[2,400,256]{2,1,0:T(8,128)(2,1)S(1)} %get-tuple-element.60.refs_5_), channel_id=1, source_target_pairs={{0,2},{1,3},{2,4},{3,5},{4,6},{5,7},{6,8},{7,9},{8,10},{9,11},{10,... | collective-permute-start | bytes 1228808 | tf_op jit(solution)/shard_map/z_relay2/ppermute | solution.py:21
  67.9 9.5 %collective-permute-start.16 = (bf16[384,384]{1,0:T(8,128)(2,1)S(1)}, bf16[384,384]{1,0:T(8,128)(2,1)S(1)}, u32[]{:S(2)}, u32[]{:S(2)}) collective-permute-start(bf16[384,384]{1,0:T(8,128)(2,1)S(1)} %get-tuple-element.64), channel_id=1, source_target_pairs={{0,64},{16,80},{32,96},{48,112},{64,128},{80,144},{96,160},{112,17... | collective-permute-start | bytes 884744 | tf_op jit(solution)/shard_map/x_main1/ppermute | solution.py:31
  69.3 8.0 %collective-permute-start.17 = (bf16[384,384]{1,0:T(8,128)(2,1)S(1)}, bf16[384,384]{1,0:T(8,128)(2,1)S(1)}, u32[]{:S(2)}, u32[]{:S(2)}) collective-permute-start(bf16[384,384]{1,0:T(8,128)(2,1)S(1)} %get-tuple-element.65), channel_id=1, source_target_pairs={{0,192},{16,208},{32,224},{48,240},{64,0},{80,16},{96,32},{112,48}... | collective-permute-start | bytes 884744 | tf_op jit(solution)/shard_map/x_main1/ppermute | solution.py:31
  77.6 18.2 %collective-permute-start.26 = (bf16[2,384,384]{2,1,0:T(8,128)(2,1)S(1)}, bf16[2,384,384]{2,1,0:T(8,128)(2,1)S(1)}, u32[]{:S(2)}, u32[]{:S(2)}) collective-permute-start(bf16[2,384,384]{2,1,0:T(8,128)(2,1)S(1)} %get-tuple-element.75), channel_id=1, source_target_pairs={{0,192},{16,208},{32,224},{48,240},{64,0},{80,16},{96,32},{112,48}... | collective-permute-start | bytes 1769480 | tf_op jit(solution)/shard_map/x_main2/ppermute | solution.py:31
  80.0 9.8 %collective-permute-start.18 = (bf16[2,400,256]{2,1,0:T(8,128)(2,1)S(1)}, bf16[2,400,256]{2,1,0:T(8,128)(2,1)S(1)}, u32[]{:S(2)}, u32[]{:S(2)}) collective-permute-start(bf16[2,400,256]{2,1,0:T(8,128)(2,1)S(1)} %get-tuple-element.67), channel_id=1, source_target_pairs={{0,2},{1,3},{2,4},{3,5},{4,6},{5,7},{6,8},{7,9},{8,10},{9,11},{10,... | collective-permute-start | bytes 1228808 | tf_op jit(solution)/shard_map/z_relay3/ppermute | solution.py:21
  80.1 9.7 %collective-permute-start.19 = (bf16[2,400,256]{2,1,0:T(8,128)(2,1)S(1)}, bf16[2,400,256]{2,1,0:T(8,128)(2,1)S(1)}, u32[]{:S(2)}, u32[]{:S(2)}) collective-permute-start(bf16[2,400,256]{2,1,0:T(8,128)(2,1)S(1)} %get-tuple-element.68), channel_id=1, source_target_pairs={{0,14},{1,15},{2,0},{3,1},{4,2},{5,3},{6,4},{7,5},{8,6},{9,7},{10,... | collective-permute-start | bytes 1228808 | tf_op jit(solution)/shard_map/z_relay3/ppermute | solution.py:21
  83.3 13.8 %collective-permute-start.25 = (bf16[2,384,384]{2,1,0:T(8,128)(2,1)S(1)}, bf16[2,384,384]{2,1,0:T(8,128)(2,1)S(1)}, u32[]{:S(2)}, u32[]{:S(2)}) collective-permute-start(bf16[2,384,384]{2,1,0:T(8,128)(2,1)S(1)} %get-tuple-element.66.refs_4_), channel_id=1, source_target_pairs={{0,64},{16,80},{32,96},{48,112},{64,128},{80,144},{96,160},{112,17... | collective-permute-start | bytes 1769480 | tf_op jit(solution)/shard_map/x_main2/ppermute | solution.py:31
  90.0 14.4 %collective-permute-start.21 = (bf16[2,400,256]{2,1,0:T(8,128)(2,1)S(1)}, bf16[2,400,256]{2,1,0:T(8,128)(2,1)S(1)}, u32[]{:S(2)}, u32[]{:S(2)}) collective-permute-start(bf16[2,400,256]{2,1,0:T(8,128)(2,1)S(1)} %get-tuple-element.70), channel_id=1, source_target_pairs={{0,14},{1,15},{2,0},{3,1},{4,2},{5,3},{6,4},{7,5},{8,6},{9,7},{10,... | collective-permute-start | bytes 1228808 | tf_op jit(solution)/shard_map/z_relay4/ppermute | solution.py:21
  93.1 11.3 %collective-permute-start.20 = (bf16[2,400,256]{2,1,0:T(8,128)(2,1)S(1)}, bf16[2,400,256]{2,1,0:T(8,128)(2,1)S(1)}, u32[]{:S(2)}, u32[]{:S(2)}) collective-permute-start(bf16[2,400,256]{2,1,0:T(8,128)(2,1)S(1)} %get-tuple-element.69.refs_2_), channel_id=1, source_target_pairs={{0,2},{1,3},{2,4},{3,5},{4,6},{5,7},{6,8},{7,9},{8,10},{9,11},{10,... | collective-permute-start | bytes 1228808 | tf_op jit(solution)/shard_map/z_relay4/ppermute | solution.py:21
  97.3 10.5 %collective-permute-start.28 = (bf16[384,384]{1,0:T(8,128)(2,1)S(1)}, bf16[384,384]{1,0:T(8,128)(2,1)S(1)}, u32[]{:S(2)}, u32[]{:S(2)}) collective-permute-start(bf16[384,384]{1,0:T(8,128)(2,1)S(1)} %get-tuple-element.76.refs_4_), channel_id=1, source_target_pairs={{0,32},{16,48},{32,0},{48,16},{64,96},{80,112},{96,64},{112,80},{1... | collective-permute-start | bytes 884744 | tf_op jit(solution)/shard_map/yh_main/ppermute | solution.py:35
  102.4 8.0 %collective-permute-start.29 = (bf16[384,384]{1,0:T(8,128)(2,1)S(1)}, bf16[384,384]{1,0:T(8,128)(2,1)S(1)}, u32[]{:S(2)}, u32[]{:S(2)}) collective-permute-start(bf16[384,384]{1,0:T(8,128)(2,1)S(1)} %get-tuple-element.77.refs_4_), channel_id=1, source_target_pairs={{0,64},{16,80},{32,96},{48,112},{64,128},{80,144},{96,160},{112,17... | collective-permute-start | bytes 884744 | tf_op jit(solution)/shard_map/x_rest2/ppermute | solution.py:31
  104.5 7.4 %collective-permute-start.27 = (bf16[400,256]{1,0:T(8,128)(2,1)S(1)}, bf16[400,256]{1,0:T(8,128)(2,1)S(1)}, u32[]{:S(2)}, u32[]{:S(2)}) collective-permute-start(bf16[400,256]{1,0:T(8,128)(2,1)S(1)} %get-tuple-element.79.refs_6_), channel_id=1, source_target_pairs={{0,1},{1,0},{2,3},{3,2},{4,5},{5,4},{6,7},{7,6},{8,9},{9,8},{10,11... | collective-permute-start | bytes 614408 | tf_op jit(solution)/shard_map/y_tokens/ppermute | solution.py:25
  (14 other events, 93.2 us)
where the time goes:
time: 113 us
  starting transfers between devices  45.7 us (40%)
  waiting for transfers between devices  31.8 us (28%)
  Pallas kernels  24.7 us (22%)
  local copies, waits for them, and re-layouts  9.98 us (9%)
    ppermute x17, starting transfers between devices, z_step(): return lax.ppermute(values, 'mp', pairs)  30.7 us
    pallas_call x19, Pallas kernels, call(): pl.pallas_call(body, in_specs=specs + [anywhere] * len(deps), out_specs=[...  24.7 us
    ppermute x17, waiting for transfers between devices, z_step(): return lax.ppermute(values, 'mp', pairs)  21.6 us
    ppermute x8, starting transfers between devices, x_step(): return lax.ppermute(values, 'dp', pairs)  10.8 us
    reshape x1, local copies, waits for them, and re-layouts, gather_tokens(): w = w_qkv.reshape(-1, GROUP, *w_qkv.shape[1:]).swapaxes(1, 2)  8.97 us
    ppermute x8, waiting for transfers between devices, x_step(): return lax.ppermute(values, 'dp', pairs)  8.27 us
    ppermute x2, starting transfers between devices, yl_swap(): return lax.ppermute(values, 'mp', [(i, i ^ 1) for i in range(Z * YL)])  2.73 us
  transfers between devices with their start and end apart: 31, of which 13 were waited for; matrix products, arithmetic and copies ran while one was open for 8% of the time, Pallas kernels for 19%

commit v1 on v0

--- a/solution.py
+++ b/solution.py
@@ -138,7 +138,7 @@
         if s == 3:
             out, sems = [(w.shape, BF)], [pltpu.SemaphoreType.DMA((Z,))]
             deps = [blocks[2]]
-            w = call(load, out, w, deps=deps, hbm=[0], limit=46, scratch=sems)[0]
+            w = call(load, out, w, deps=deps, hbm=[0], limit=44, scratch=sems)[0]
             blocks[s] = tie([blocks[s]], w, 1)[0]
     blocks[FAR] = z_step(blocks[FAR + 1], 1)
     return [blocks[d] for d in range(Z)], w, tokens
@@ -468,16 +468,17 @@
     bwd_ref[half:] = wide_sum(own_ref[2, half:], got_ref[2, half:], b_ref[...]).astype(BF)
 
 
-def finish_weight(mine_ref, got_ref, own_ref, other_ref, f_ref, b_ref, out_ref, done_ref):
+def finish_main(mine_ref, got_ref, out_ref):
+    out_ref[...] = wide_sum(mine_ref[...], got_ref[...]).T
+
+
+def finish_weight(main_ref, own_ref, other_ref, f_ref, b_ref, out_ref, done_ref):
     done_ref[...] = jnp.zeros_like(done_ref)
-    main, n3 = mine_ref.shape[0], out_ref.shape[2]
-    parts = [
-        wide_sum(mine_ref[...], got_ref[...]),
-        wide_sum(own_ref[3], other_ref[3], f_ref[...], b_ref[...]),
-    ]
-    whole = jnp.concatenate(parts, 0)
+    n3 = out_ref.shape[2]
+    rest = wide_sum(own_ref[3], other_ref[3], f_ref[...], b_ref[...]).T
+    whole = jnp.concatenate([main_ref[...], rest], 1)
     for h in range(out_ref.shape[1]):
-        out_ref[:, h, :] = whole[h * n3 : (h + 1) * n3].T
+        out_ref[:, h, :] = whole[:, h * n3 : (h + 1) * n3]
 
 
 def local(tokens, ln_gain, w_qkv, q_gain, k_gain, d_out):
@@ -558,7 +559,8 @@
         got_y = yl_swap(to_other)
     with jax.named_scope("weight_out"):
         shape = [((width, heads, n3), F32, None), ((8, 128), F32)]
-        operands = [mine, got, r_own, r_got, r_fwd, r_bwd]
+        main_out = call(finish_main, [((width, main), F32)], mine, got, deps=[to_other])[0]
+        operands = [main_out, r_own, r_got, r_fwd, r_bwd]
         grad_weight, done = call(finish_weight, shape, *operands, deps=[to_other])
     with jax.named_scope("tokens_out"):
         shape = [((rows, width), BF, None)]

time: 113 us -> 113 us (level)
    pallas_call x19 -> x20, Pallas kernels: 24.7 us -> 24.8 us  [call(): pl.pallas_call(body, in_specs=specs + [anywhere] * len(deps), out_specs=[...]
where the time goes in v1:
time: 113 us
  starting transfers between devices  45.7 us (40%)
  waiting for transfers between devices  32.6 us (29%)
  Pallas kernels  24.8 us (22%)
  local copies, waits for them, and re-layouts  9.01 us (8%)
    ppermute x17, starting transfers between devices, z_step(): return lax.ppermute(values, 'mp', pairs)  30.7 us
    pallas_call x20, Pallas kernels, call(): pl.pallas_call(body, in_specs=specs + [anywhere] * len(deps), out_specs=[...  24.8 us
    ppermute x17, waiting for transfers between devices, z_step(): return lax.ppermute(values, 'mp', pairs)  22.6 us
    ppermute x8, starting transfers between devices, x_step(): return lax.ppermute(values, 'dp', pairs)  10.8 us
    reshape x1, local copies, waits for them, and re-layouts, gather_tokens(): w = w_qkv.reshape(-1, GROUP, *w_qkv.shape[1:]).swapaxes(1, 2)  8.98 us
    ppermute x8, waiting for transfers between devices, x_step(): return lax.ppermute(values, 'dp', pairs)  8 us
    ppermute x2, starting transfers between devices, yl_swap(): return lax.ppermute(values, 'mp', [(i, i ^ 1) for i in range(Z * YL)])  2.74 us
  transfers between devices with their start and end apart: 31, of which 13 were waited for; matrix products, arithmetic and copies ran while one was open for 8% of the time, Pallas kernels for 19%

profile of v1, /device:TPU:16, one launch (start us, length us, event | category | flops | bytes accessed | tf_op | source)
XLA Modules:
  0.0 112.9 jit_solution(10445239119468424592)
XLA Ops:
  2.0 5.9 %collective-permute-start.3 = (bf16[256,384]{1,0:T(8,128)(2,1)}, bf16[256,384]{1,0:T(8,128)(2,1)S(1)}, u32[]{:S(2)}, u32[]{:S(2)}) collective-permute-start(bf16[256,384]{1,0:T(8,128)(2,1)} %refs_0_.1), channel_id=1, source_target_pairs={{0,14},{1,15},{2,0},{3,1},{4,2},{5,3},{6,4},{7,5},{8,6},{9,7},{10,... | collective-permute-start | bytes 589832 | tf_op jit(solution)/shard_map/gather/ppermute | solution.py:21
  7.9 5.6 %collective-permute-start.4 = (bf16[256,384]{1,0:T(8,128)(2,1)S(1)}, bf16[256,384]{1,0:T(8,128)(2,1)S(1)}, u32[]{:S(2)}, u32[]{:S(2)}) collective-permute-start(bf16[256,384]{1,0:T(8,128)(2,1)S(1)} %collective-permute-done.refs_3_.refs_1_), channel_id=1, source_target_pairs={{0,14},{1,15},{2,0},{3,1},{4,2},{5,3},{6,4},{7,5},{8,6},{9,7},{10,... | collective-permute-start | bytes 589832 | tf_op jit(solution)/shard_map/gather/ppermute | solution.py:21
  16.7 3.6 %collective-permute-done.2.refs_1_ = bf16[256,384]{1,0:T(8,128)(2,1)S(1)} collective-permute-done((bf16[256,384]{1,0:T(8,128)(2,1)S(1)}, bf16[256,384]{1,0:T(8,128)(2,1)S(1)}, u32[]{:S(2)}, u32[]{:S(2)}) %collective-permute-start.2) | collective-permute-done | bytes 196640 | tf_op jit(solution)/shard_map/gather/ppermute | solution.py:21
  20.5 3.2 %collective-permute-start.6 = (bf16[2,256,384]{2,1,0:T(8,128)(2,1)S(1)}, bf16[2,256,384]{2,1,0:T(8,128)(2,1)S(1)}, u32[]{:S(2)}, u32[]{:S(2)}) collective-permute-start(bf16[2,256,384]{2,1,0:T(8,128)(2,1)S(1)} %get-tuple-element.44.refs_2_.refs_1_), channel_id=1, source_target_pairs={{0,14},{1,15},{2,0},{3,1},{4,2},{5,3},{6,4},{7,5},{8,6},{9,7},{10,... | collective-permute-start | bytes 1179656 | tf_op jit(solution)/shard_map/gather/ppermute | solution.py:21
  23.7 9.0 %copy.17 = bf16[384,16,2,384]{3,1,2,0:T(8,128)(2,1)} copy(bf16[384,16,2,384]{3,2,1,0:T(2,128)(2,1)} %bitcast.13) | data formatting | bytes 18874368 | tf_op jit(solution)/shard_map/gather/reshape | solution.py:132
  32.8 3.2 %collective-permute-start.7 = (bf16[2,256,384]{2,1,0:T(8,128)(2,1)S(1)}, bf16[2,256,384]{2,1,0:T(8,128)(2,1)S(1)}, u32[]{:S(2)}, u32[]{:S(2)}) collective-permute-start(bf16[2,256,384]{2,1,0:T(8,128)(2,1)S(1)} %get-tuple-element.46.refs_1_.refs_2_), channel_id=1, source_target_pairs={{0,14},{1,15},{2,0},{3,1},{4,2},{5,3},{6,4},{7,5},{8,6},{9,7},{10,... | collective-permute-start | bytes 1179656 | tf_op jit(solution)/shard_map/gather/ppermute | solution.py:21
  36.1 6.0 %collective-permute-done.8.refs_4_.refs_5_ = bf16[2,256,384]{2,1,0:T(8,128)(2,1)S(1)} collective-permute-done((bf16[2,256,384]{2,1,0:T(8,128)(2,1)S(1)}, bf16[2,256,384]{2,1,0:T(8,128)(2,1)S(1)}, u32[]{:S(2)}, u32[]{:S(2)}) %collective-permute-start.8) | collective-permute-done | bytes 393248 | tf_op jit(solution)/shard_map/gather/ppermute | solution.py:21
  42.2 3.8 %load.1.refs_1_.refs_8_.refs_9_.refs_4_ = bf16[384,2,16,384]{3,2,1,0:T(8,128)(2,1)S(1)} custom-call(bf16[384,2,16,384]{3,2,1,0:T(8,128)(2,1)} %bitcast.12, bf16[2,256,384]{2,1,0:T(8,128)(2,1)S(1)} %get-tuple-element.46.refs_1_.refs_2_), custom_call_target="tpu_custom_call" | custom-call | flops 1024 | bytes 1024 | tf_op jit(solution)/shard_map/gather/load/pallas_call | solution.py:75
  46.0 3.6 %project_near.1 = (f32[256,768]{1,0:T(8,128)S(1)}, f32[16,768]{1,0:T(8,128)S(1)}, f32[256,128]{1,0:T(8,128)S(1)}) custom-call(bf16[2,256,384]{2,1,0:T(8,128)(2,1)S(1)} %pair.3.refs_0_, bf16[2,256,384]{2,1,0:T(8,128)(2,1)S(1)} %get-tuple-element.44.refs_2_.refs_1_, bf16[2,256,384]{2,1,0:T(8,128)(2,1)S(1)} %get-tuple-element.46.refs_1_.refs_2_, ...), custom_call_target="tpu_custom_call" | custom-call | flops 1024 | bytes 1024 | tf_op jit(solution)/shard_map/project_near/pallas_call | solution.py:75
  51.1 2.3 %project.1 = (f32[256,768]{1,0:T(8,128)S(1)}, bf16[8,256,384]{2,1,0:T(8,128)(2,1)S(1)}, bf16[8,256,384]{2,1,0:T(8,128)(2,1)S(1)}, f32[8,256]{1,0:T(8,128)S(1)}) custom-call(bf16[2,256,384]{2,1,0:T(8,128)(2,1)S(1)} %pair.3.refs_0_, bf16[2,256,384]{2,1,0:T(8,128)(2,1)S(1)} %get-tuple-element.44.refs_2_.refs_1_, ...), custom_call_target="tpu_custom_call" | custom-call | flops 1024 | bytes 1024 | tf_op jit(solution)/shard_map/project/pallas_call | solution.py:75
  53.5 2.4 %attend.1 = (bf16[256,256]{1,0:T(8,128)(2,1)}, bf16[768,256]{1,0:T(8,128)(2,1)S(1)}, f32[8,256]{1,0:T(8,128)S(1)}, bf16[400,256]{1,0:T(8,128)(2,1)S(1)}, bf16[400,256]{1,0:T(8,128)(2,1)S(1)}) custom-call(f32[256,768]{1,0:T(8,128)S(1)} %get-tuple-element.51.refs_0_, f32[16,768]{1,0:T(8,128)S(1)} %get-tuple-element.49.refs_11_.refs_1_, ...), custom_call_target="tpu_custom_call" | custom-call | flops 1024 | bytes 1024 | tf_op jit(solution)/shard_map/attend/pallas_call | solution.py:75
  56.4 3.2 %collective-permute-start.13 = (bf16[400,256]{1,0:T(8,128)(2,1)S(1)}, bf16[400,256]{1,0:T(8,128)(2,1)S(1)}, u32[]{:S(2)}, u32[]{:S(2)}) collective-permute-start(bf16[400,256]{1,0:T(8,128)(2,1)S(1)} %get-tuple-element.58), channel_id=1, source_target_pairs={{0,14},{1,15},{2,0},{3,1},{4,2},{5,3},{6,4},{7,5},{8,6},{9,7},{10,... | collective-permute-start | bytes 614408 | tf_op jit(solution)/shard_map/z_relay1/ppermute | solution.py:21
  59.7 2.0 %first_terms.1 = (bf16[384,384]{1,0:T(8,128)(2,1)S(1)}, bf16[384,384]{1,0:T(8,128)(2,1)S(1)}, bf16[4,384,384]{2,1,0:T(8,128)(2,1)S(1)}, bf16[2,768,256]{2,1,0:T(8,128)(2,1)S(1)}) custom-call(bf16[8,256,384]{2,1,0:T(8,128)(2,1)S(1)} %get-tuple-element.53.refs_0_, bf16[8,256,384]{2,1,0:T(8,128)(2,1)S(1)} %collective-permute-done.10.refs_1_, ...), custom_call_target="tpu_custom_call" | custom-call | flops 1024 | bytes 1024 | tf_op jit(solution)/shard_map/first_terms/pallas_call | solution.py:75
  62.1 2.5 %collective-permute-done.12.refs_1_ = bf16[400,256]{1,0:T(8,128)(2,1)S(1)} collective-permute-done((bf16[400,256]{1,0:T(8,128)(2,1)S(1)}, bf16[400,256]{1,0:T(8,128)(2,1)S(1)}, u32[]{:S(2)}, u32[]{:S(2)}) %collective-permute-start.12) | collective-permute-done | bytes 204832 | tf_op jit(solution)/shard_map/z_relay1/ppermute | solution.py:21
  64.8 3.0 %collective-permute-start.15 = (bf16[2,400,256]{2,1,0:T(8,128)(2,1)S(1)}, bf16[2,400,256]{2,1,0:T(8,128)(2,1)S(1)}, u32[]{:S(2)}, u32[]{:S(2)}) collective-permute-start(bf16[2,400,256]{2,1,0:T(8,128)(2,1)S(1)} %get-tuple-element.62), channel_id=1, source_target_pairs={{0,14},{1,15},{2,0},{3,1},{4,2},{5,3},{6,4},{7,5},{8,6},{9,7},{10,... | collective-permute-start | bytes 1228808 | tf_op jit(solution)/shard_map/z_relay2/ppermute | solution.py:21
  71.0 6.2 %later_terms.1 = (bf16[6,384,384]{2,1,0:T(8,128)(2,1)S(1)}, bf16[4,384,384]{2,1,0:T(8,128)(2,1)S(1)}, bf16[5,768,256]{2,1,0:T(8,128)(2,1)S(1)}) custom-call(bf16[8,256,384]{2,1,0:T(8,128)(2,1)S(1)} %get-tuple-element.53.refs_0_, bf16[8,256,384]{2,1,0:T(8,128)(2,1)S(1)} %collective-permute-done.10.refs_1_, bf16[768,256]{1,0:T(8,128)(2,1)S(1)} %get-tuple-element.55.refs_2_, ...), custom_call_target="tpu_custom_call" | custom-call | flops 1024 | bytes 1024 | tf_op jit(solution)/shard_map/later_terms/pallas_call | solution.py:75
  77.5 2.2 %collective-permute-start.26 = (bf16[2,384,384]{2,1,0:T(8,128)(2,1)S(1)}, bf16[2,384,384]{2,1,0:T(8,128)(2,1)S(1)}, u32[]{:S(2)}, u32[]{:S(2)}) collective-permute-start(bf16[2,384,384]{2,1,0:T(8,128)(2,1)S(1)} %get-tuple-element.75), channel_id=1, source_target_pairs={{0,192},{16,208},{32,224},{48,240},{64,0},{80,16},{96,32},{112,48}... | collective-permute-start | bytes 1769480 | tf_op jit(solution)/shard_map/x_main2/ppermute | solution.py:31
  80.0 3.2 %collective-permute-start.19 = (bf16[2,400,256]{2,1,0:T(8,128)(2,1)S(1)}, bf16[2,400,256]{2,1,0:T(8,128)(2,1)S(1)}, u32[]{:S(2)}, u32[]{:S(2)}) collective-permute-start(bf16[2,400,256]{2,1,0:T(8,128)(2,1)S(1)} %get-tuple-element.68), channel_id=1, source_target_pairs={{0,14},{1,15},{2,0},{3,1},{4,2},{5,3},{6,4},{7,5},{8,6},{9,7},{10,... | collective-permute-start | bytes 1228808 | tf_op jit(solution)/shard_map/z_relay3/ppermute | solution.py:21
  84.0 5.8 %collective-permute-done.18.refs_1_ = bf16[2,400,256]{2,1,0:T(8,128)(2,1)S(1)} collective-permute-done((bf16[2,400,256]{2,1,0:T(8,128)(2,1)S(1)}, bf16[2,400,256]{2,1,0:T(8,128)(2,1)S(1)}, u32[]{:S(2)}, u32[]{:S(2)}) %collective-permute-start.18) | collective-permute-done | bytes 409632 | tf_op jit(solution)/shard_map/z_relay3/ppermute | solution.py:21
  89.9 3.1 %collective-permute-start.21 = (bf16[2,400,256]{2,1,0:T(8,128)(2,1)S(1)}, bf16[2,400,256]{2,1,0:T(8,128)(2,1)S(1)}, u32[]{:S(2)}, u32[]{:S(2)}) collective-permute-start(bf16[2,400,256]{2,1,0:T(8,128)(2,1)S(1)} %get-tuple-element.70), channel_id=1, source_target_pairs={{0,14},{1,15},{2,0},{3,1},{4,2},{5,3},{6,4},{7,5},{8,6},{9,7},{10,... | collective-permute-start | bytes 1228808 | tf_op jit(solution)/shard_map/z_relay4/ppermute | solution.py:21
  93.1 2.5 %collective-permute-start.24 = (bf16[192,384]{1,0:T(8,128)(2,1)S(1)}, bf16[192,384]{1,0:T(8,128)(2,1)S(1)}, u32[]{:S(2)}, u32[]{:S(2)}) collective-permute-start(bf16[192,384]{1,0:T(8,128)(2,1)S(1)} %get-tuple-element.74), channel_id=1, source_target_pairs={{0,192},{16,208},{32,224},{48,240},{64,0},{80,16},{96,32},{112,48}... | collective-permute-start | bytes 442376 | tf_op jit(solution)/shard_map/x_rest1/ppermute | solution.py:31
  98.4 3.6 %collective-permute-done.23.refs_2_ = bf16[192,384]{1,0:T(8,128)(2,1)S(1)} collective-permute-done((bf16[192,384]{1,0:T(8,128)(2,1)S(1)}, bf16[192,384]{1,0:T(8,128)(2,1)S(1)}, u32[]{:S(2)}, u32[]{:S(2)}) %collective-permute-start.23) | collective-permute-done | bytes 147488 | tf_op jit(solution)/shard_map/x_rest1/ppermute | solution.py:31
  102.3 2.0 %collective-permute-start.29 = (bf16[384,384]{1,0:T(8,128)(2,1)S(1)}, bf16[384,384]{1,0:T(8,128)(2,1)S(1)}, u32[]{:S(2)}, u32[]{:S(2)}) collective-permute-start(bf16[384,384]{1,0:T(8,128)(2,1)S(1)} %get-tuple-element.77.refs_4_), channel_id=1, source_target_pairs={{0,64},{16,80},{32,96},{48,112},{64,128},{80,144},{96,160},{112,17... | collective-permute-start | bytes 884744 | tf_op jit(solution)/shard_map/x_rest2/ppermute | solution.py:31
  105.8 2.0 %collective-permute-done.28.refs_1_ = bf16[384,384]{1,0:T(8,128)(2,1)S(1)} collective-permute-done((bf16[384,384]{1,0:T(8,128)(2,1)S(1)}, bf16[384,384]{1,0:T(8,128)(2,1)S(1)}, u32[]{:S(2)}, u32[]{:S(2)}) %collective-permute-start.28) | collective-permute-done | bytes 294944 | tf_op jit(solution)/shard_map/yh_main/ppermute | solution.py:35
  (73 shorter events, 21.9 us)
Async XLA Ops:
  2.0 11.4 %collective-permute-start.3 = (bf16[256,384]{1,0:T(8,128)(2,1)}, bf16[256,384]{1,0:T(8,128)(2,1)S(1)}, u32[]{:S(2)}, u32[]{:S(2)}) collective-permute-start(bf16[256,384]{1,0:T(8,128)(2,1)} %refs_0_.1), channel_id=1, source_target_pairs={{0,14},{1,15},{2,0},{3,1},{4,2},{5,3},{6,4},{7,5},{8,6},{9,7},{10,... | collective-permute-start | bytes 589832 | tf_op jit(solution)/shard_map/gather/ppermute | solution.py:21
  7.9 7.5 %collective-permute-start.1 = (bf16[256,384]{1,0:T(8,128)(2,1)}, bf16[256,384]{1,0:T(8,128)(2,1)S(1)}, u32[]{:S(2)}, u32[]{:S(2)}) collective-permute-start(bf16[256,384]{1,0:T(8,128)(2,1)} %refs_0_.1), channel_id=1, source_target_pairs={{0,2},{1,3},{2,4},{3,5},{4,6},{5,7},{6,8},{7,9},{8,10},{9,11},{10,... | collective-permute-start | bytes 589832 | tf_op jit(solution)/shard_map/gather/ppermute | solution.py:21
  7.9 8.9 %collective-permute-start.4 = (bf16[256,384]{1,0:T(8,128)(2,1)S(1)}, bf16[256,384]{1,0:T(8,128)(2,1)S(1)}, u32[]{:S(2)}, u32[]{:S(2)}) collective-permute-start(bf16[256,384]{1,0:T(8,128)(2,1)S(1)} %collective-permute-done.refs_3_.refs_1_), channel_id=1, source_target_pairs={{0,14},{1,15},{2,0},{3,1},{4,2},{5,3},{6,4},{7,5},{8,6},{9,7},{10,... | collective-permute-start | bytes 589832 | tf_op jit(solution)/shard_map/gather/ppermute | solution.py:21
  20.4 12.3 %collective-permute-start.5 = (bf16[2,256,384]{2,1,0:T(8,128)(2,1)S(1)}, bf16[2,256,384]{2,1,0:T(8,128)(2,1)S(1)}, u32[]{:S(2)}, u32[]{:S(2)}) collective-permute-start(bf16[2,256,384]{2,1,0:T(8,128)(2,1)S(1)} %get-tuple-element.45.refs_6_.refs_7_), channel_id=1, source_target_pairs={{0,2},{1,3},{2,4},{3,5},{4,6},{5,7},{6,8},{7,9},{8,10},{9,11},{10,... | collective-permute-start | bytes 1179656 | tf_op jit(solution)/shard_map/gather/ppermute | solution.py:21
  20.5 12.2 %collective-permute-start.6 = (bf16[2,256,384]{2,1,0:T(8,128)(2,1)S(1)}, bf16[2,256,384]{2,1,0:T(8,128)(2,1)S(1)}, u32[]{:S(2)}, u32[]{:S(2)}) collective-permute-start(bf16[2,256,384]{2,1,0:T(8,128)(2,1)S(1)} %get-tuple-element.44.refs_2_.refs_1_), channel_id=1, source_target_pairs={{0,14},{1,15},{2,0},{3,1},{4,2},{5,3},{6,4},{7,5},{8,6},{9,7},{10,... | collective-permute-start | bytes 1179656 | tf_op jit(solution)/shard_map/gather/ppermute | solution.py:21
  32.7 9.4 %collective-permute-start.8 = (bf16[2,256,384]{2,1,0:T(8,128)(2,1)S(1)}, bf16[2,256,384]{2,1,0:T(8,128)(2,1)S(1)}, u32[]{:S(2)}, u32[]{:S(2)}) collective-permute-start(bf16[2,256,384]{2,1,0:T(8,128)(2,1)S(1)} %get-tuple-element.47.refs_5_.refs_6_), channel_id=1, source_target_pairs={{0,2},{1,3},{2,4},{3,5},{4,6},{5,7},{6,8},{7,9},{8,10},{9,11},{10,... | collective-permute-start | bytes 1179656 | tf_op jit(solution)/shard_map/gather/ppermute | solution.py:21
  32.8 13.2 %collective-permute-start.7 = (bf16[2,256,384]{2,1,0:T(8,128)(2,1)S(1)}, bf16[2,256,384]{2,1,0:T(8,128)(2,1)S(1)}, u32[]{:S(2)}, u32[]{:S(2)}) collective-permute-start(bf16[2,256,384]{2,1,0:T(8,128)(2,1)S(1)} %get-tuple-element.46.refs_1_.refs_2_), channel_id=1, source_target_pairs={{0,14},{1,15},{2,0},{3,1},{4,2},{5,3},{6,4},{7,5},{8,6},{9,7},{10,... | collective-permute-start | bytes 1179656 | tf_op jit(solution)/shard_map/gather/ppermute | solution.py:21
  42.1 9.0 %collective-permute-start.9 = (bf16[2,256,384]{2,1,0:T(8,128)(2,1)S(1)}, bf16[2,256,384]{2,1,0:T(8,128)(2,1)S(1)}, u32[]{:S(2)}, u32[]{:S(2)}) collective-permute-start(bf16[2,256,384]{2,1,0:T(8,128)(2,1)S(1)} %collective-permute-done.8.refs_4_.refs_5_), channel_id=1, source_target_pairs={{0,2},{1,3},{2,4},{3,5},{4,6},{5,7},{6,8},{7,9},{8,10},{9,11},{10,... | collective-permute-start | bytes 1179656 | tf_op jit(solution)/shard_map/gather/ppermute | solution.py:21
  56.4 8.2 %collective-permute-start.12 = (bf16[400,256]{1,0:T(8,128)(2,1)S(1)}, bf16[400,256]{1,0:T(8,128)(2,1)S(1)}, u32[]{:S(2)}, u32[]{:S(2)}) collective-permute-start(bf16[400,256]{1,0:T(8,128)(2,1)S(1)} %get-tuple-element.57), channel_id=1, source_target_pairs={{0,2},{1,3},{2,4},{3,5},{4,6},{5,7},{6,8},{7,9},{8,10},{9,11},{10,... | collective-permute-start | bytes 614408 | tf_op jit(solution)/shard_map/z_relay1/ppermute | solution.py:21
  56.4 8.2 %collective-permute-start.13 = (bf16[400,256]{1,0:T(8,128)(2,1)S(1)}, bf16[400,256]{1,0:T(8,128)(2,1)S(1)}, u32[]{:S(2)}, u32[]{:S(2)}) collective-permute-start(bf16[400,256]{1,0:T(8,128)(2,1)S(1)} %get-tuple-element.58), channel_id=1, source_target_pairs={{0,14},{1,15},{2,0},{3,1},{4,2},{5,3},{6,4},{7,5},{8,6},{9,7},{10,... | collective-permute-start | bytes 614408 | tf_op jit(solution)/shard_map/z_relay1/ppermute | solution.py:21
  61.7 31.4 %collective-permute-start.22 = (bf16[4,384,384]{2,1,0:T(8,128)(2,1)S(1)}, bf16[4,384,384]{2,1,0:T(8,128)(2,1)S(1)}, u32[]{:S(2)}, u32[]{:S(2)}) collective-permute-start(bf16[4,384,384]{2,1,0:T(8,128)(2,1)S(1)} %get-tuple-element.72), channel_id=1, source_target_pairs={{0,32},{16,48},{32,0},{48,16},{64,96},{80,112},{96,64},{112,80},{1... | collective-permute-start | bytes 3538952 | tf_op jit(solution)/shard_map/yh_rest/ppermute | solution.py:35
  64.8 15.0 %collective-permute-start.15 = (bf16[2,400,256]{2,1,0:T(8,128)(2,1)S(1)}, bf16[2,400,256]{2,1,0:T(8,128)(2,1)S(1)}, u32[]{:S(2)}, u32[]{:S(2)}) collective-permute-start(bf16[2,400,256]{2,1,0:T(8,128)(2,1)S(1)} %get-tuple-element.62), channel_id=1, source_target_pairs={{0,14},{1,15},{2,0},{3,1},{4,2},{5,3},{6,4},{7,5},{8,6},{9,7},{10,... | collective-permute-start | bytes 1228808 | tf_op jit(solution)/shard_map/z_relay2/ppermute | solution.py:21
  67.8 11.9 %collective-permute-start.14 = (bf16[2,400,256]{2,1,0:T(8,128)(2,1)S(1)}, bf16[2,400,256]{2,1,0:T(8,128)(2,1)S(1)}, u32[]{:S(2)}, u32[]{:S(2)}) collective-permute-start(bf16[2,400,256]{2,1,0:T(8,128)(2,1)S(1)} %get-tuple-element.60.refs_5_), channel_id=1, source_target_pairs={{0,2},{1,3},{2,4},{3,5},{4,6},{5,7},{6,8},{7,9},{8,10},{9,11},{10,... | collective-permute-start | bytes 1228808 | tf_op jit(solution)/shard_map/z_relay2/ppermute | solution.py:21
  67.8 9.5 %collective-permute-start.16 = (bf16[384,384]{1,0:T(8,128)(2,1)S(1)}, bf16[384,384]{1,0:T(8,128)(2,1)S(1)}, u32[]{:S(2)}, u32[]{:S(2)}) collective-permute-start(bf16[384,384]{1,0:T(8,128)(2,1)S(1)} %get-tuple-element.64), channel_id=1, source_target_pairs={{0,64},{16,80},{32,96},{48,112},{64,128},{80,144},{96,160},{112,17... | collective-permute-start | bytes 884744 | tf_op jit(solution)/shard_map/x_main1/ppermute | solution.py:31
  69.3 8.0 %collective-permute-start.17 = (bf16[384,384]{1,0:T(8,128)(2,1)S(1)}, bf16[384,384]{1,0:T(8,128)(2,1)S(1)}, u32[]{:S(2)}, u32[]{:S(2)}) collective-permute-start(bf16[384,384]{1,0:T(8,128)(2,1)S(1)} %get-tuple-element.65), channel_id=1, source_target_pairs={{0,192},{16,208},{32,224},{48,240},{64,0},{80,16},{96,32},{112,48}... | collective-permute-start | bytes 884744 | tf_op jit(solution)/shard_map/x_main1/ppermute | solution.py:31
  77.5 18.1 %collective-permute-start.26 = (bf16[2,384,384]{2,1,0:T(8,128)(2,1)S(1)}, bf16[2,384,384]{2,1,0:T(8,128)(2,1)S(1)}, u32[]{:S(2)}, u32[]{:S(2)}) collective-permute-start(bf16[2,384,384]{2,1,0:T(8,128)(2,1)S(1)} %get-tuple-element.75), channel_id=1, source_target_pairs={{0,192},{16,208},{32,224},{48,240},{64,0},{80,16},{96,32},{112,48}... | collective-permute-start | bytes 1769480 | tf_op jit(solution)/shard_map/x_main2/ppermute | solution.py:31
  79.9 9.8 %collective-permute-start.18 = (bf16[2,400,256]{2,1,0:T(8,128)(2,1)S(1)}, bf16[2,400,256]{2,1,0:T(8,128)(2,1)S(1)}, u32[]{:S(2)}, u32[]{:S(2)}) collective-permute-start(bf16[2,400,256]{2,1,0:T(8,128)(2,1)S(1)} %get-tuple-element.67), channel_id=1, source_target_pairs={{0,2},{1,3},{2,4},{3,5},{4,6},{5,7},{6,8},{7,9},{8,10},{9,11},{10,... | collective-permute-start | bytes 1228808 | tf_op jit(solution)/shard_map/z_relay3/ppermute | solution.py:21
  80.0 9.7 %collective-permute-start.19 = (bf16[2,400,256]{2,1,0:T(8,128)(2,1)S(1)}, bf16[2,400,256]{2,1,0:T(8,128)(2,1)S(1)}, u32[]{:S(2)}, u32[]{:S(2)}) collective-permute-start(bf16[2,400,256]{2,1,0:T(8,128)(2,1)S(1)} %get-tuple-element.68), channel_id=1, source_target_pairs={{0,14},{1,15},{2,0},{3,1},{4,2},{5,3},{6,4},{7,5},{8,6},{9,7},{10,... | collective-permute-start | bytes 1228808 | tf_op jit(solution)/shard_map/z_relay3/ppermute | solution.py:21
  83.3 13.8 %collective-permute-start.25 = (bf16[2,384,384]{2,1,0:T(8,128)(2,1)S(1)}, bf16[2,384,384]{2,1,0:T(8,128)(2,1)S(1)}, u32[]{:S(2)}, u32[]{:S(2)}) collective-permute-start(bf16[2,384,384]{2,1,0:T(8,128)(2,1)S(1)} %get-tuple-element.66.refs_4_), channel_id=1, source_target_pairs={{0,64},{16,80},{32,96},{48,112},{64,128},{80,144},{96,160},{112,17... | collective-permute-start | bytes 1769480 | tf_op jit(solution)/shard_map/x_main2/ppermute | solution.py:31
  89.9 14.3 %collective-permute-start.21 = (bf16[2,400,256]{2,1,0:T(8,128)(2,1)S(1)}, bf16[2,400,256]{2,1,0:T(8,128)(2,1)S(1)}, u32[]{:S(2)}, u32[]{:S(2)}) collective-permute-start(bf16[2,400,256]{2,1,0:T(8,128)(2,1)S(1)} %get-tuple-element.70), channel_id=1, source_target_pairs={{0,14},{1,15},{2,0},{3,1},{4,2},{5,3},{6,4},{7,5},{8,6},{9,7},{10,... | collective-permute-start | bytes 1228808 | tf_op jit(solution)/shard_map/z_relay4/ppermute | solution.py:21
  93.1 11.2 %collective-permute-start.20 = (bf16[2,400,256]{2,1,0:T(8,128)(2,1)S(1)}, bf16[2,400,256]{2,1,0:T(8,128)(2,1)S(1)}, u32[]{:S(2)}, u32[]{:S(2)}) collective-permute-start(bf16[2,400,256]{2,1,0:T(8,128)(2,1)S(1)} %get-tuple-element.69.refs_2_), channel_id=1, source_target_pairs={{0,2},{1,3},{2,4},{3,5},{4,6},{5,7},{6,8},{7,9},{8,10},{9,11},{10,... | collective-permute-start | bytes 1228808 | tf_op jit(solution)/shard_map/z_relay4/ppermute | solution.py:21
  97.3 10.5 %collective-permute-start.28 = (bf16[384,384]{1,0:T(8,128)(2,1)S(1)}, bf16[384,384]{1,0:T(8,128)(2,1)S(1)}, u32[]{:S(2)}, u32[]{:S(2)}) collective-permute-start(bf16[384,384]{1,0:T(8,128)(2,1)S(1)} %get-tuple-element.76.refs_4_), channel_id=1, source_target_pairs={{0,32},{16,48},{32,0},{48,16},{64,96},{80,112},{96,64},{112,80},{1... | collective-permute-start | bytes 884744 | tf_op jit(solution)/shard_map/yh_main/ppermute | solution.py:35
  102.3 8.0 %collective-permute-start.29 = (bf16[384,384]{1,0:T(8,128)(2,1)S(1)}, bf16[384,384]{1,0:T(8,128)(2,1)S(1)}, u32[]{:S(2)}, u32[]{:S(2)}) collective-permute-start(bf16[384,384]{1,0:T(8,128)(2,1)S(1)} %get-tuple-element.77.refs_4_), channel_id=1, source_target_pairs={{0,64},{16,80},{32,96},{48,112},{64,128},{80,144},{96,160},{112,17... | collective-permute-start | bytes 884744 | tf_op jit(solution)/shard_map/x_rest2/ppermute | solution.py:31
  104.5 7.3 %collective-permute-start.27 = (bf16[400,256]{1,0:T(8,128)(2,1)S(1)}, bf16[400,256]{1,0:T(8,128)(2,1)S(1)}, u32[]{:S(2)}, u32[]{:S(2)}) collective-permute-start(bf16[400,256]{1,0:T(8,128)(2,1)S(1)} %get-tuple-element.79.refs_2_.refs_5_), channel_id=1, source_target_pairs={{0,1},{1,0},{2,3},{3,2},{4,5},{5,4},{6,7},{7,6},{8,9},{9,8},{10,11... | collective-permute-start | bytes 614408 | tf_op jit(solution)/shard_map/y_tokens/ppermute | solution.py:25
  (12 other events, 82.6 us)
